TPU v7x, 32 devices: a whole 2x2x4 slice. The times are simulated.
32 devices in a mesh: maps: 2 (over y), row: 4 (over x, core), col: 4 (over z).
Axes of the slice: x: 2, y: 2, z: 4, core: 2. Of those that a mesh axis runs over, the one named last changes fastest.
Arguments:
- positions: float32 [512, 2, 384], P(('maps', 'row', 'col')), parts along dimension 0, may hold values from 0 to 127
- destination: int32 [512, 1], P(('maps', 'row', 'col')), parts along dimension 0, may hold values from 0 to 15; in each aligned block of 16 rows (0 to 15, 16 to 31, ...) at most 4 rows name the same one
- profile: float32 [65, 65], replicated, may hold values from 0.03 to 1
Outputs:
- magnification: float32 [1024, 512], P(('maps', 'row'), 'col'), parts along dimension 0
There are 2 independent parts, one for each index of `maps`. A program takes and returns all parts, laid end to end along the dimension named above; an argument that names none is the same for every part. Nothing has to cross between parts.
Inputs may be any that keep to these rules, and one draw needn't show every extreme that they name: `destination`: at most 4 of the blocks of one device name one tile.
All inputs are finite; a program needn't handle non-finite values.
Results may differ from a plain program's by a relative error of at most 0.0003.
Values may be sent and summed in bfloat16 or wider, within the bound.
No kernel may reach another device: no remote copies, remote signals or barrier semaphores. Data moves between devices by JAX's collectives and lax.ppermute only.
A program may use at most 64 MiB of HBM per device.

v0:
```python
import functools

import jax
import jax.numpy as jnp
from jax import lax
from jax.experimental import pallas as pl
from jax.experimental.pallas import tpu as pltpu
from jax.sharding import PartitionSpec as P

TILE = 128
HALO = 32
MOST = 4
DISC = 2 * HALO + 1
STEP = 16
LONG = TILE + STEP
TURNS = 2 * HALO // STEP
WIDE = TILE + 2 * HALO
LANES = 128
SPAN = 64
BATCH = 8
ROOM = 5
COUNT = 16
ROWS = 32
COLS = 64
FAR = 1024.0

VMEM = pl.BlockSpec(memory_space=pltpu.VMEM)
SMEM = pl.BlockSpec(memory_space=pltpu.SMEM)
ALONE = pltpu.CompilerParams(vmem_limit_bytes=67_104_000)
LIMIT = pltpu.CompilerParams(vmem_limit_bytes=32 * 1024 * 1024)


def touches(distance, least, most):
    before = (distance == -1.0) & (most > TILE - HALO - 1.0)
    after = (distance == 1.0) & (least < HALO)
    return (distance == 0.0) | before | after


def pack_kernel(turn_ref, dest_ref, rays_ref, out_ref, labels, parts):
    blocks, _, rays = rays_ref.shape
    tiles = out_ref.shape[0] // 8
    width = parts.shape[0]
    col_count = lax.axis_size("col")
    skip = 0.0 if turn_ref is None else 2.0 * ROOM * turn_ref[0].astype(jnp.float32)
    lane = lax.broadcasted_iota(jnp.int32, (blocks, width), 1)
    place = lax.broadcasted_iota(jnp.int32, (blocks, width), 0)
    there = (lane % blocks == place) & (lane < 3 * blocks)

    def laid(column):
        return jnp.sum(jnp.where(there, column, 0.0), axis=0, keepdims=True)

    labels[...] = jnp.full(labels.shape, -1.0, jnp.float32)
    for g in range(3):
        labels[0:1, g * blocks : (g + 1) * blocks] = dest_ref[...].astype(jnp.float32)
    label = labels[...]
    label_row = jnp.floor((label + 0.5) / col_count)
    label_col = label - label_row * col_count
    first, second = rays_ref[:, 0, :], rays_ref[:, 1, :]
    least_row, most_row = laid(jnp.min(first, 1, keepdims=True)), laid(jnp.max(first, 1, keepdims=True))
    least_col, most_col = laid(jnp.min(second, 1, keepdims=True)), laid(jnp.max(second, 1, keepdims=True))
    earlier = lax.broadcasted_iota(jnp.int32, (width, width), 0)
    later = lax.broadcasted_iota(jnp.int32, (width, width), 1)
    earlier = jnp.where((earlier < later % blocks) & (later < 3 * blocks), 1.0, 0.0).astype(jnp.bfloat16)

    def chosen(tile):
        odd = (tile // col_count % 2).astype(jnp.float32)
        row = (tile // col_count).astype(jnp.float32) - odd
        dc = label_col - (tile % col_count).astype(jnp.float32)
        aside = touches(dc, least_col, most_col) & (label >= 0.0)

        def coded(dr):
            reach = aside & touches(dr, least_row, most_row)
            return reach, jnp.where(reach, jnp.where(dr == 0.0, 0.0, 2.0) + jnp.where(dc == 0.0, 0.0, 1.0), FAR), dr

        even, odds = coded(label_row - row), coded(label_row - row - 1.0)
        reach = jnp.where(even[0] | odds[0], 1.0, 0.0)
        rank = jnp.dot(reach.astype(jnp.bfloat16), earlier, preferred_element_type=jnp.float32)
        left = rank - skip - odd
        slot = jnp.floor(left * 0.5)
        mine = (reach > 0.0) & (slot * 2.0 == left) & (slot >= 0.0) & (slot < ROOM)
        return jnp.where(mine, slot, -1.0), even, odds, dc, (rank + 1.0) * reach

    slot, even, odds, dc, most = chosen(lax.broadcasted_iota(jnp.int32, (tiles, width), 0))
    most = jnp.max(jnp.max(most, axis=1, keepdims=True), axis=0, keepdims=True)
    turns = jnp.floor((most + (2.0 * ROOM - 0.5)) / (2.0 * ROOM))
    lane = lax.broadcasted_iota(jnp.int32, (tiles, width), 1)
    meta = jnp.where(lane == COUNT, turns, FAR)
    for k in range(ROOM):
        here = (slot == k) & (lane < blocks)
        columns = [(COLS + k, dc * (2.0 * TILE)), (COLS + 8 + k, dc * (2.0 * TILE))]
        for at, (_, kind, dr) in ((k, even), (8 + k, odds)):
            columns += [(at, kind), (ROWS + at, dr * (2.0 * TILE))]
        for at, value in columns:
            found = jnp.sum(jnp.where(here, value - FAR, 0.0), axis=1, keepdims=True) + FAR
            meta = jnp.where(lane == at, found, meta)

    parts[...] = jnp.zeros(parts.shape, jnp.float32)
    parts[:blocks, :rays] = first
    parts[:blocks, rays:] = second[:, :LANES]
    parts[blocks : 2 * blocks, : 2 * LANES] = second[:, LANES:]
    parts[2 * blocks : 3 * blocks, 2 * LANES :] = second[:, LANES:]
    parts[3 * blocks : 3 * blocks + tiles, 2 * LANES : 3 * LANES] = meta[:, :LANES]

    row = lax.broadcasted_iota(jnp.int32, (8 * tiles, width), 0)
    group = lax.broadcasted_iota(jnp.int32, (8 * tiles, width), 1)
    slot = chosen(row // 8)[0]
    within = row % 8
    low = (2 * (within - ROOM)).astype(jnp.float32)
    head = (group < blocks) & (within < ROOM) & (slot == within.astype(jnp.float32))
    even = (group >= blocks) & (group < 2 * blocks) & (within >= ROOM) & (slot == low)
    uneven = (group >= 2 * blocks) & (group < 3 * blocks) & (within >= ROOM) & (slot == low + 1.0)
    codes = (group - 3 * blocks == row // 8) & (group >= 3 * blocks) & (within == 7)
    select = jnp.where(head | even | uneven | codes, 1.0, 0.0).astype(jnp.bfloat16)
    rest = parts[...]
    total = jnp.zeros(out_ref.shape, jnp.float32)
    for _ in range(3):
        part = rest.astype(jnp.bfloat16)
        rest = rest - part.astype(jnp.float32)
        total = total + jnp.dot(select, part, preferred_element_type=jnp.float32)
    out_ref[...] = total


def build_table(profile_ref, pairs_ref, last_ref):
    a = lax.broadcasted_iota(jnp.int32, (DISC, DISC), 0) - HALO
    c = lax.broadcasted_iota(jnp.int32, (DISC, DISC), 1) - HALO
    weights = jnp.where(a * a + c * c <= HALO * HALO, profile_ref[...], 0.0)
    kernel = (weights / jnp.sum(weights)).astype(jnp.bfloat16)
    source = lax.broadcasted_iota(jnp.int32, (DISC, LANES), 0)
    target = lax.broadcasted_iota(jnp.int32, (DISC, LANES), 1)
    mirror = jnp.where((source + target) % LANES == 0, 1.0, 0.0).astype(jnp.bfloat16)
    mirrored = jnp.dot(kernel, mirror, preferred_element_type=jnp.float32)
    left = lax.broadcasted_iota(jnp.int32, (LANES, LANES), 1) < SPAN

    def band(row, start):
        wide = jnp.broadcast_to(mirrored[row : row + 1, :], (LANES, LANES))
        return pltpu.roll(wide, start, 1, stride=1, stride_axis=0)

    for u in range(TURNS):
        for s in range(0, STEP, 2):
            row = u * STEP + s
            both = jnp.where(left, band(row, 0), band(row + 1, SPAN))
            pairs_ref[u * LANES : (u + 1) * LANES, s * SPAN : (s + 2) * SPAN] = both.astype(jnp.bfloat16)
    last_ref[...] = jnp.where(left, band(2 * HALO, 0), 0.0).astype(jnp.bfloat16)


def hats(row, cell):
    near, far, here, there = (value.astype(jnp.bfloat16) for value in row)
    zero = jnp.zeros((), jnp.bfloat16)
    return jnp.where(cell == here, near, jnp.where(cell == there, far, zero))


def deposited(both, build, lists, stage, shifts, facts):
    sources = both.shape[0]
    rays = 3 * LANES
    first_lane = lax.axis_index("row") % 2 * 8
    room = sources * ROOM + 1
    kinds = both[:, 7, 2 * LANES :][:, :LANES]
    lane = lax.broadcasted_iota(jnp.int32, (sources, LANES), 1) - first_lane
    source = lax.broadcasted_iota(jnp.int32, (sources, LANES), 0)
    power = (1 << jnp.clip(lane + source % 4 * ROOM, 0, 23)).astype(jnp.float32)
    power = jnp.where((lane >= 0) & (lane < ROOM), power, 0.0)

    def bits(chosen):
        held = jnp.where(chosen, power, 0.0)
        return [jnp.sum(held[at : at + 4]).astype(jnp.int32) for at in range(0, sources, 4)]

    reached, outer = bits(kinds < 4.0), bits((kinds == 2.0) | (kinds == 3.0))
    beside = bits((kinds == 1.0) | (kinds == 3.0))
    masks = [
        [r & ~(o | b) for r, o, b in zip(reached, outer, beside)],
        [b & ~o for o, b in zip(outer, beside)],
        [o & ~b for o, b in zip(outer, beside)],
        [o & b for o, b in zip(outer, beside)],
    ]
    def listed(counts, slots):
        counts = list(counts)
        for kind in range(4):
            for at in range(sources):
                for k in slots:
                    lists[kind * room + counts[kind]] = at * 8 + k
                    bit = (masks[kind][at // 4] >> (at % 4 * ROOM + k)) & 1
                    counts[kind] = counts[kind] + bit
        return tuple(counts)

    build()
    rare = sum(1 << (at * ROOM + k) for at in range(4) for k in range(3, ROOM))
    seldom = functools.reduce(jnp.bitwise_or, reached) & rare
    counts = listed((jnp.int32(0),) * 4, range(3))
    counts = lax.cond(seldom != 0, lambda held: listed(held, range(3, ROOM)), lambda held: held, counts)
    for kind in range(4):
        lists[kind * room + counts[kind]] = ROOM

    def doubled(cell):
        return (2 * cell).astype(jnp.float32).astype(jnp.bfloat16)

    own = doubled(lax.broadcasted_iota(jnp.int32, (TILE, rays), 0))
    edge = lax.broadcasted_iota(jnp.int32, (2 * HALO, rays), 0)
    edge = doubled(jnp.where(edge < HALO, edge - HALO, edge + (TILE - HALO)))
    lane = lax.broadcasted_iota(jnp.int32, (1, LANES), 1) - first_lane

    def load(kind, step, batch, start):
        for k in range(batch):
            at = start + k
            entry = lists[kind * room + jnp.minimum(step * batch + k, counts[kind])]
            source, slot = entry >> 3, entry & 7
            head = both[source, pl.ds(slot, 1), :]
            tail = both[source, pl.ds(ROOM + (slot >> 1), 1), :]
            meta = both[source, 7:8, :][:, 2 * LANES : 3 * LANES]
            stage[0, at : at + 1, :] = head[:, :rays]
            stage[1, at : at + 1, :LANES] = head[:, rays:]
            stage[1, at : at + 1, LANES:] = jnp.where(
                (slot & 1) == 1, tail[:, 2 * LANES :], tail[:, : 2 * LANES]
            )
            shifts[0, at : at + 1, :] = jnp.where(lane == slot + ROWS, meta, 0.0)
            shifts[1, at : at + 1, :] = jnp.where(lane == slot + COLS, meta, 0.0)

    def prepare(begin, end):
        for axis in range(2):
            coords = stage[axis, begin:end, :]
            low = jnp.floor(coords)
            facts[4 * axis, begin:end, :] = 1.0 - (coords - low)
            facts[4 * axis + 1, begin:end, :] = 1.0 - ((low + 1.0) - coords)
            here = 2.0 * low + jnp.sum(shifts[axis, begin:end, :], axis=1, keepdims=True)
            facts[4 * axis + 2, begin:end, :] = here
            facts[4 * axis + 3, begin:end, :] = here + 2.0

    def product(kind, batch, start):
        down, across = (own, edge)[kind // 2], (own, edge)[kind % 2]
        firsts, seconds = [], []
        for at in range(start, start + batch):
            row = [facts[j, at : at + 1, :] for j in range(8)]
            firsts.append(hats(row[:4], down))
            seconds.append(hats(row[4:], across))
        return lax.dot_general(
            jnp.concatenate(firsts, axis=1),
            jnp.concatenate(seconds, axis=1),
            (((1,), (1,)), ((), ())),
            preferred_element_type=jnp.float32,
        )

    def together(one, two):
        def ready(step, *given):
            for kind, batch, start in given:
                load(kind, step, batch, start)
            prepare(given[0][2], given[-1][2] + 8)

        def step_one(step, sums, given=one):
            sums = sums + product(*given)
            ready(step + 1, given)
            return sums

        def step_both(step, sums):
            sums = sums[0] + product(*one), sums[1] + product(*two)
            ready(step + 1, one, two)
            return sums

        ready(0, one, two)
        zeros = [
            jnp.zeros(((TILE, 2 * HALO)[kind // 2], (TILE, 2 * HALO)[kind % 2]), jnp.float32)
            for kind in (one[0], two[0])
        ]
        steps = [(counts[kind] + batch - 1) // batch for kind, batch, _ in (one, two)]
        shared = jnp.minimum(steps[0], steps[1])
        sums = lax.fori_loop(0, shared, step_both, tuple(zeros))
        return [
            lax.fori_loop(shared, steps[j], functools.partial(step_one, given=(one, two)[j]), sums[j])
            for j in range(2)
        ]

    inside, corners = together((0, BATCH, 0), (3, BATCH // 2, BATCH))
    beside, above = together((1, BATCH // 2, 0), (2, BATCH // 2, BATCH))

    def wide(middle, ends):
        return jnp.concatenate([ends[:, :HALO], middle, ends[:, HALO:]], axis=1)

    middle, ends = wide(inside, beside), wide(above, corners)
    return jnp.concatenate([ends[:HALO], middle, ends[HALO:]], axis=0)


def spread_kernel(scale, mine_ref, other_ref, profile_ref, dest_ref, rays_ref, before_ref, out_ref,
                  total_ref, dest_copy, rays_copy, pairs_ref, last_ref, left, both, *scratch):
    sources = mine_ref.shape[0]
    both[:sources] = mine_ref[...]
    both[sources:] = other_ref[...]
    dest_copy[...] = dest_ref[...]
    rays_copy[...] = rays_ref[...]
    build = functools.partial(build_table, profile_ref, pairs_ref, last_ref)
    cells = deposited(both, build, *scratch)
    if before_ref is not None:
        cells = cells + before_ref[...]
    total_ref[...] = cells
    blocks = [cells[:, at : at + LANES].astype(jnp.bfloat16) for at in (0, SPAN)]
    for h in range(2):
        for u in range(TURNS):
            left[h * LONG : (h + 1) * LONG, u * LANES : (u + 1) * LANES] = blocks[h][
                u * STEP : u * STEP + LONG, :
            ]
    lowest = jnp.concatenate([block[2 * HALO :, :] for block in blocks], axis=0)
    ends = jnp.dot(lowest, last_ref[...], preferred_element_type=jnp.float32)
    evens = [ends[:TILE], ends[TILE:]]
    odds = [jnp.zeros((TILE, LANES), jnp.float32)] * 2
    for p in range(0, STEP * SPAN, 2 * LANES):
        both = jnp.dot(left[...], pairs_ref[:, p : p + 2 * LANES], preferred_element_type=jnp.float32)
        for h in range(2):
            for lanes in (0, LANES):
                s = (p + lanes) // SPAN
                part = both[h * LONG : (h + 1) * LONG, lanes : lanes + LANES]
                evens[h] = evens[h] + part[s : s + TILE]
                odds[h] = odds[h] + part[s + 1 : s + 1 + TILE]
    low = evens[0] + pltpu.roll(odds[0], SPAN, 1)
    high = pltpu.roll(evens[1], SPAN, 1) + odds[1]
    lane = lax.broadcasted_iota(jnp.int32, (TILE, LANES), 1)
    out_ref[...] = jnp.where(lane < SPAN, low, high) / scale


def shards(positions, destination, profile):
    blocks, _, rays = positions.shape
    row_count, col_count = lax.axis_size("row"), lax.axis_size("col")
    tiles = row_count * col_count
    width = -(-(3 * blocks + tiles) // LANES) * LANES

    def exchange(turn, labels, coords):
        kernel, given = pack_kernel, (turn, labels, coords)
        if turn is None:
            kernel, given = functools.partial(pack_kernel, None), (labels, coords)
        outgoing = pl.pallas_call(
            kernel,
            out_shape=jax.ShapeDtypeStruct((8 * tiles, rays + LANES), jnp.float32),
            in_specs=[SMEM, VMEM, VMEM][-len(given) :],
            out_specs=VMEM,
            scratch_shapes=[
                pltpu.VMEM((1, width), jnp.float32),
                pltpu.VMEM((width, rays + LANES), jnp.float32),
            ],
            compiler_params=ALONE if turn is None else LIMIT,
            name="pack",
        )(*given)
        return lax.all_to_all(
            outgoing.reshape(tiles, 8, rays + LANES), ("row", "col"), split_axis=0, concat_axis=0, tiled=True
        )

    def deposit(mine, labels, coords, before):
        other = lax.ppermute(mine, "row", [(i, i ^ 1) for i in range(row_count)])
        scale = blocks * rays / (TILE * TILE)
        kernel, given = functools.partial(spread_kernel, scale), (mine, other, profile, labels, coords, before)
        if before is None:
            kernel = lambda *refs: spread_kernel(scale, *refs[:5], None, *refs[5:])
            given = given[:5]
        return pl.pallas_call(
            kernel,
            out_shape=(
                jax.ShapeDtypeStruct((TILE, TILE), jnp.float32),
                jax.ShapeDtypeStruct((WIDE, WIDE), jnp.float32),
                jax.ShapeDtypeStruct((1, blocks), jnp.int32),
                jax.ShapeDtypeStruct(positions.shape, jnp.float32),
            ),
            in_specs=[VMEM] * len(given),
            out_specs=(VMEM,) * 4,
            scratch_shapes=[
                pltpu.VMEM((TURNS * LANES, STEP * SPAN), jnp.bfloat16),
                pltpu.VMEM((LANES, LANES), jnp.bfloat16),
                pltpu.VMEM((2 * LONG, TURNS * LANES), jnp.bfloat16),
                pltpu.VMEM((2 * tiles, 8, rays + LANES), jnp.float32),
                pltpu.SMEM((4 * (2 * tiles * ROOM + 1),), jnp.int32),
                pltpu.VMEM((2, 2 * BATCH, rays), jnp.float32),
                pltpu.VMEM((2, 2 * BATCH, LANES), jnp.float32),
                pltpu.VMEM((8, 2 * BATCH, rays), jnp.float32),
            ],
            compiler_params=LIMIT,
            name="spread",
        )(*given)

    mine = exchange(None, destination.T, positions)
    turns = jnp.max(mine[:, 7, 2 * LANES + COUNT]).astype(jnp.int32)
    out, total, labels, coords = deposit(mine, destination.T, positions, None)

    def more(state):
        turn, _, total, labels, coords = state
        mine = exchange(jnp.full((1,), turn, jnp.int32), labels, coords)
        return (turn + 1, *deposit(mine, labels, coords, total))

    state = (jnp.int32(1), out, total, labels, coords)
    return lax.while_loop(lambda state: state[0] < turns, more, state)[1]


def solution(mesh):
    placed = (P(("maps", "row", "col"), None, None), P(("maps", "row", "col"), None), P())
    return jax.shard_map(
        shards, mesh=mesh, in_specs=placed, out_specs=P(("maps", "row"), "col"), check_vma=False
    )
```

profile of v0, /device:TPU:1, one launch (start us, length us, event | category | flops | bytes accessed | tf_op | source)
XLA Modules:
  0.0 27.7 jit_solution(13889071155227824077)
XLA Ops:
  0.0 2.2 %pack.2 = f32[128,512]{1,0:T(8,128)} custom-call(s32[1,16]{1,0:T(1,128)} %bitcast.9, f32[16,2,384]{2,1,0:T(2,128)} %refs_4_.1), custom_call_target="tpu_custom_call" | custom-call | tf_op jit(solution)/shard_map/pack/pallas_call | solution.py:326
  2.2 0.0 copy-start
  2.2 0.0 copy-start.2
  2.2 16.8 %all_to_all.11.refs_0_ = f32[16,8,512]{2,1,0:T(8,128)S(1)} all-to-all(f32[16,8,512]{2,1,0:T(8,128)} %bitcast.11), channel_id=1, replica_groups=mesh['maps'=2,'row'=4,'col'=4] {'row','col'}, dimensions={0} | all-to-all | bytes 524288 | tf_op jit(solution)/shard_map/all_to_all | solution.py:338
  19.0 0.8 %collective-permute-start.1 = (f32[16,8,512]{2,1,0:T(8,128)S(1)}, f32[16,8,512]{2,1,0:T(8,128)S(1)}, u32[]{:S(2)}, u32[]{:S(2)}) collective-permute-start(f32[16,8,512]{2,1,0:T(8,128)S(1)} %all_to_all.11.refs_0_), channel_id=1, source_target_pairs={{0,4},{4,0},{8,12},{12,8},{1,5},{5,1},{9,13},{13,9},{2,6},{6,2},{1... | collective-permute-start | bytes 786440 | tf_op jit(solution)/shard_map/ppermute | solution.py:343
  19.8 0.7 %slice_reduce_fusion = f32[]{:T(128)} fusion(f32[16,8,512]{2,1,0:T(8,128)S(1)} %all_to_all.11.refs_0_), kind=kLoop, calls=%fused_computation | loop fusion | flops 15 | bytes 68 | tf_op jit(solution)/shard_map/reduce_max | solution.py:374
  20.5 0.0 copy-start.1
  21.2 0.0 collective-permute-done.1.refs_1_
  21.2 0.0 copy-done
  21.2 0.0 copy-done.2
  21.2 0.0 copy-done.1
  21.2 6.4 %spread.2 = (f32[128,128]{1,0:T(8,128)}, f32[192,192]{1,0:T(8,128)S(1)}, s32[1,16]{1,0:T(1,128)S(1)}, f32[16,2,384]{2,1,0:T(2,128)S(1)}) custom-call(f32[16,8,512]{2,1,0:T(8,128)S(1)} %all_to_all.11.refs_0_, f32[16,8,512]{2,1,0:T(8,128)S(1)} %collective-permute-done.1.refs_1_, f32[65,65]{1,0:T(8,128)S(1)} %copy-done.2, s32[1,16]{1,0:T(1,128)S(1)} %bitcast.10, ...), custom_call_target="tpu_custom_call" | custom-call | tf_op jit(solution)/shard_map/spread/pallas_call | solution.py:349
  (1 shorter events, 0.0 us)
Async XLA Ops:
  2.2 19.0 %copy-start = (f32[16,2,384]{2,1,0:T(2,128)S(1)}, f32[16,2,384]{2,1,0:T(2,128)}, u32[]{:S(2)}) copy-start(f32[16,2,384]{2,1,0:T(2,128)} %refs_4_.1) | copy-start | bytes 147460
  2.2 19.0 %copy-start.2 = (f32[65,65]{1,0:T(8,128)S(1)}, f32[65,65]{1,0:T(8,128)}, u32[]{:S(2)}) copy-start(f32[65,65]{1,0:T(8,128)} %refs_2_.1) | copy-start | bytes 50704
  19.0 2.2 %collective-permute-start.1 = (f32[16,8,512]{2,1,0:T(8,128)S(1)}, f32[16,8,512]{2,1,0:T(8,128)S(1)}, u32[]{:S(2)}, u32[]{:S(2)}) collective-permute-start(f32[16,8,512]{2,1,0:T(8,128)S(1)} %all_to_all.11.refs_0_), channel_id=1, source_target_pairs={{0,4},{4,0},{8,12},{12,8},{1,5},{5,1},{9,13},{13,9},{2,6},{6,2},{1... | collective-permute-start | bytes 786440 | tf_op jit(solution)/shard_map/ppermute | solution.py:343
  20.5 0.7 %copy-start.1 = (s32[16,1]{0,1:T(1,128)S(1)}, s32[16,1]{0,1:T(1,128)}, u32[]{:S(2)}) copy-start(s32[16,1]{0,1:T(1,128)} %param.6) | copy-start | bytes 196
where the time goes:
time: 27.8 us; the launch traced here: 27.7 us
  blocking collectives  16.8 us (60%)
  Pallas kernels  8.64 us (31%)
  starting transfers between devices  0.82 us (3%)
  between operations  0.7 us (3%)
  other arithmetic  0.69 us (2%)
    all_to_all x1, blocking collectives, exchange(): lax.all_to_all(outgoing.reshape(tiles, 8, rays + LANES), ('row', 'col'),...  16.8 us
    pallas_call x1, Pallas kernels, deposit(): pl.pallas_call(kernel, out_shape=(jax.ShapeDtypeStruct((TILE, TILE), jnp....  6.41 us
    pallas_call x1, Pallas kernels, exchange(): pl.pallas_call(kernel, out_shape=jax.ShapeDtypeStruct((8 * tiles, rays +...  2.23 us
    ppermute x1, starting transfers between devices, deposit(): other = lax.ppermute(mine, 'row', [(i, i ^ 1) for i in range(row_count)])  0.82 us
    reduce_max x1, other arithmetic, shards(): turns = jnp.max(mine[:, 7, 2 * LANES + COUNT]).astype(jnp.int32)  0.69 us
  transfers between devices with their start and end apart: 1, of which 0 were waited for; matrix products, arithmetic and copies ran while one was open for 2% of the time, Pallas kernels for 0%

commit v1 on v0

--- a/solution.py
+++ b/solution.py
@@ -20,13 +20,10 @@
 BATCH = 8
 ROOM = 5
 COUNT = 16
-ROWS = 32
-COLS = 64
 FAR = 1024.0
 
 VMEM = pl.BlockSpec(memory_space=pltpu.VMEM)
 SMEM = pl.BlockSpec(memory_space=pltpu.SMEM)
-ALONE = pltpu.CompilerParams(vmem_limit_bytes=67_104_000)
 LIMIT = pltpu.CompilerParams(vmem_limit_bytes=32 * 1024 * 1024)
 
 
@@ -36,28 +33,47 @@
     return (distance == 0.0) | before | after
 
 
-def pack_kernel(turn_ref, dest_ref, rays_ref, out_ref, labels, parts):
+def lay_kernel(rays_ref, parts_ref, bounds_ref):
     blocks, _, rays = rays_ref.shape
-    tiles = out_ref.shape[0] // 8
-    width = parts.shape[0]
-    col_count = lax.axis_size("col")
-    skip = 0.0 if turn_ref is None else 2.0 * ROOM * turn_ref[0].astype(jnp.float32)
+    width = bounds_ref.shape[1]
     lane = lax.broadcasted_iota(jnp.int32, (blocks, width), 1)
     place = lax.broadcasted_iota(jnp.int32, (blocks, width), 0)
     there = (lane % blocks == place) & (lane < 3 * blocks)
-
-    def laid(column):
-        return jnp.sum(jnp.where(there, column, 0.0), axis=0, keepdims=True)
-
+    first, second = rays_ref[:, 0, :], rays_ref[:, 1, :]
+    for row, column in enumerate(
+        (
+            jnp.min(first, 1, keepdims=True),
+            jnp.max(first, 1, keepdims=True),
+            jnp.min(second, 1, keepdims=True),
+            jnp.max(second, 1, keepdims=True),
+        )
+    ):
+        bounds_ref[row : row + 1, :] = jnp.sum(jnp.where(there, column, 0.0), axis=0, keepdims=True)
+    parts = parts_ref.at[0]
+    parts_ref[...] = jnp.zeros(parts_ref.shape, jnp.bfloat16)
+    for part in range(3):
+        one, two = first.astype(jnp.bfloat16), second.astype(jnp.bfloat16)
+        first, second = first - one.astype(jnp.float32), second - two.astype(jnp.float32)
+        parts = parts_ref.at[part]
+        parts[:blocks, :rays] = one
+        parts[:blocks, rays:] = two[:, :LANES]
+        parts[blocks : 2 * blocks, : 2 * LANES] = two[:, LANES:]
+        parts[2 * blocks : 3 * blocks, 2 * LANES :] = two[:, LANES:]
+
+
+def pack_kernel(turn_ref, dest_ref, parts_ref, bounds_ref, out_ref, labels):
+    blocks = dest_ref.shape[1]
+    tiles = out_ref.shape[0] // 8
+    width = parts_ref.shape[1]
+    col_count = lax.axis_size("col")
+    skip = 0.0 if turn_ref is None else 2.0 * ROOM * turn_ref[0].astype(jnp.float32)
     labels[...] = jnp.full(labels.shape, -1.0, jnp.float32)
     for g in range(3):
         labels[0:1, g * blocks : (g + 1) * blocks] = dest_ref[...].astype(jnp.float32)
     label = labels[...]
     label_row = jnp.floor((label + 0.5) / col_count)
     label_col = label - label_row * col_count
-    first, second = rays_ref[:, 0, :], rays_ref[:, 1, :]
-    least_row, most_row = laid(jnp.min(first, 1, keepdims=True)), laid(jnp.max(first, 1, keepdims=True))
-    least_col, most_col = laid(jnp.min(second, 1, keepdims=True)), laid(jnp.max(second, 1, keepdims=True))
+    least_row, most_row, least_col, most_col = (bounds_ref[j : j + 1, :] for j in range(4))
     earlier = lax.broadcasted_iota(jnp.int32, (width, width), 0)
     later = lax.broadcasted_iota(jnp.int32, (width, width), 1)
     earlier = jnp.where((earlier < later % blocks) & (later < 3 * blocks), 1.0, 0.0).astype(jnp.bfloat16)
@@ -70,7 +86,7 @@
 
         def coded(dr):
             reach = aside & touches(dr, least_row, most_row)
-            return reach, jnp.where(reach, jnp.where(dr == 0.0, 0.0, 2.0) + jnp.where(dc == 0.0, 0.0, 1.0), FAR), dr
+            return reach, jnp.where(reach, 3.0 * dr + dc + 4.0, FAR)
 
         even, odds = coded(label_row - row), coded(label_row - row - 1.0)
         reach = jnp.where(even[0] | odds[0], 1.0, 0.0)
@@ -78,28 +94,7 @@
         left = rank - skip - odd
         slot = jnp.floor(left * 0.5)
         mine = (reach > 0.0) & (slot * 2.0 == left) & (slot >= 0.0) & (slot < ROOM)
-        return jnp.where(mine, slot, -1.0), even, odds, dc, (rank + 1.0) * reach
-
-    slot, even, odds, dc, most = chosen(lax.broadcasted_iota(jnp.int32, (tiles, width), 0))
-    most = jnp.max(jnp.max(most, axis=1, keepdims=True), axis=0, keepdims=True)
-    turns = jnp.floor((most + (2.0 * ROOM - 0.5)) / (2.0 * ROOM))
-    lane = lax.broadcasted_iota(jnp.int32, (tiles, width), 1)
-    meta = jnp.where(lane == COUNT, turns, FAR)
-    for k in range(ROOM):
-        here = (slot == k) & (lane < blocks)
-        columns = [(COLS + k, dc * (2.0 * TILE)), (COLS + 8 + k, dc * (2.0 * TILE))]
-        for at, (_, kind, dr) in ((k, even), (8 + k, odds)):
-            columns += [(at, kind), (ROWS + at, dr * (2.0 * TILE))]
-        for at, value in columns:
-            found = jnp.sum(jnp.where(here, value - FAR, 0.0), axis=1, keepdims=True) + FAR
-            meta = jnp.where(lane == at, found, meta)
-
-    parts[...] = jnp.zeros(parts.shape, jnp.float32)
-    parts[:blocks, :rays] = first
-    parts[:blocks, rays:] = second[:, :LANES]
-    parts[blocks : 2 * blocks, : 2 * LANES] = second[:, LANES:]
-    parts[2 * blocks : 3 * blocks, 2 * LANES :] = second[:, LANES:]
-    parts[3 * blocks : 3 * blocks + tiles, 2 * LANES : 3 * LANES] = meta[:, :LANES]
+        return jnp.where(mine, slot, -1.0), even[1], odds[1], (rank + 1.0) * reach
 
     row = lax.broadcasted_iota(jnp.int32, (8 * tiles, width), 0)
     group = lax.broadcasted_iota(jnp.int32, (8 * tiles, width), 1)
@@ -109,15 +104,24 @@
     head = (group < blocks) & (within < ROOM) & (slot == within.astype(jnp.float32))
     even = (group >= blocks) & (group < 2 * blocks) & (within >= ROOM) & (slot == low)
     uneven = (group >= 2 * blocks) & (group < 3 * blocks) & (within >= ROOM) & (slot == low + 1.0)
-    codes = (group - 3 * blocks == row // 8) & (group >= 3 * blocks) & (within == 7)
-    select = jnp.where(head | even | uneven | codes, 1.0, 0.0).astype(jnp.bfloat16)
-    rest = parts[...]
-    total = jnp.zeros(out_ref.shape, jnp.float32)
-    for _ in range(3):
-        part = rest.astype(jnp.bfloat16)
-        rest = rest - part.astype(jnp.float32)
-        total = total + jnp.dot(select, part, preferred_element_type=jnp.float32)
+    select = jnp.where(head | even | uneven, 1.0, 0.0).astype(jnp.bfloat16)
+    total = jnp.dot(select, parts_ref[0], preferred_element_type=jnp.float32)
+    for part in range(1, 3):
+        total = total + jnp.dot(select, parts_ref[part], preferred_element_type=jnp.float32)
     out_ref[...] = total
+
+    slot, even, odds, most = chosen(lax.broadcasted_iota(jnp.int32, (tiles, width), 0))
+    most = jnp.max(jnp.max(most, axis=1, keepdims=True), axis=0, keepdims=True)
+    turns = jnp.floor((most + (2.0 * ROOM - 0.5)) / (2.0 * ROOM))
+    lane = lax.broadcasted_iota(jnp.int32, (tiles, width), 1)
+    meta = jnp.where(lane == COUNT, turns, FAR)
+    for k in range(ROOM):
+        here = (slot == k) & (lane < blocks)
+        for at, code in ((k, even), (8 + k, odds)):
+            found = jnp.sum(jnp.where(here, code - FAR, 0.0), axis=1, keepdims=True) + FAR
+            meta = jnp.where(lane == at, found, meta)
+    for t in range(tiles):
+        out_ref[8 * t + 7 : 8 * t + 8, 2 * LANES : 3 * LANES] = meta[t : t + 1, :LANES]
 
 
 def build_table(profile_ref, pairs_ref, last_ref):
@@ -154,18 +158,19 @@
     rays = 3 * LANES
     first_lane = lax.axis_index("row") % 2 * 8
     room = sources * ROOM + 1
-    kinds = both[:, 7, 2 * LANES :][:, :LANES]
+    code = both[:, 7, 2 * LANES :][:, :LANES]
+    rowwise = jnp.floor((code + 0.5) / 3.0)
+    held, above, aside = code < 9.0, rowwise != 1.0, code - 3.0 * rowwise != 1.0
     lane = lax.broadcasted_iota(jnp.int32, (sources, LANES), 1) - first_lane
     source = lax.broadcasted_iota(jnp.int32, (sources, LANES), 0)
     power = (1 << jnp.clip(lane + source % 4 * ROOM, 0, 23)).astype(jnp.float32)
     power = jnp.where((lane >= 0) & (lane < ROOM), power, 0.0)
 
     def bits(chosen):
-        held = jnp.where(chosen, power, 0.0)
-        return [jnp.sum(held[at : at + 4]).astype(jnp.int32) for at in range(0, sources, 4)]
-
-    reached, outer = bits(kinds < 4.0), bits((kinds == 2.0) | (kinds == 3.0))
-    beside = bits((kinds == 1.0) | (kinds == 3.0))
+        value = jnp.where(chosen, power, 0.0)
+        return [jnp.sum(value[at : at + 4]).astype(jnp.int32) for at in range(0, sources, 4)]
+
+    reached, outer, beside = bits(held), bits(held & above), bits(held & aside)
     masks = [
         [r & ~(o | b) for r, o, b in zip(reached, outer, beside)],
         [b & ~o for o, b in zip(outer, beside)],
@@ -211,16 +216,18 @@
             stage[1, at : at + 1, LANES:] = jnp.where(
                 (slot & 1) == 1, tail[:, 2 * LANES :], tail[:, : 2 * LANES]
             )
-            shifts[0, at : at + 1, :] = jnp.where(lane == slot + ROWS, meta, 0.0)
-            shifts[1, at : at + 1, :] = jnp.where(lane == slot + COLS, meta, 0.0)
+            shifts[at : at + 1, :] = jnp.where(lane == slot, meta, 0.0)
 
     def prepare(begin, end):
+        code = jnp.sum(shifts[begin:end, :], axis=1, keepdims=True)
+        rowwise = jnp.floor((code + 0.5) / 3.0)
+        offsets = (rowwise - 1.0) * (2.0 * TILE), (code - 3.0 * rowwise - 1.0) * (2.0 * TILE)
         for axis in range(2):
             coords = stage[axis, begin:end, :]
             low = jnp.floor(coords)
             facts[4 * axis, begin:end, :] = 1.0 - (coords - low)
             facts[4 * axis + 1, begin:end, :] = 1.0 - ((low + 1.0) - coords)
-            here = 2.0 * low + jnp.sum(shifts[axis, begin:end, :], axis=1, keepdims=True)
+            here = 2.0 * low + offsets[axis]
             facts[4 * axis + 2, begin:end, :] = here
             facts[4 * axis + 3, begin:end, :] = here + 2.0
 
@@ -317,22 +324,30 @@
     blocks, _, rays = positions.shape
     row_count, col_count = lax.axis_size("row"), lax.axis_size("col")
     tiles = row_count * col_count
-    width = -(-(3 * blocks + tiles) // LANES) * LANES
+    width = -(-3 * blocks // LANES) * LANES
 
     def exchange(turn, labels, coords):
-        kernel, given = pack_kernel, (turn, labels, coords)
+        laid = pl.pallas_call(
+            lay_kernel,
+            out_shape=(
+                jax.ShapeDtypeStruct((3, width, rays + LANES), jnp.bfloat16),
+                jax.ShapeDtypeStruct((4, width), jnp.float32),
+            ),
+            in_specs=[VMEM],
+            out_specs=(VMEM, VMEM),
+            compiler_params=LIMIT,
+            name="lay",
+        )(coords)
+        kernel, given = pack_kernel, (turn, labels, *laid)
         if turn is None:
-            kernel, given = functools.partial(pack_kernel, None), (labels, coords)
+            kernel, given = functools.partial(pack_kernel, None), (labels, *laid)
         outgoing = pl.pallas_call(
             kernel,
             out_shape=jax.ShapeDtypeStruct((8 * tiles, rays + LANES), jnp.float32),
-            in_specs=[SMEM, VMEM, VMEM][-len(given) :],
+            in_specs=[SMEM, VMEM, VMEM, VMEM][-len(given) :],
             out_specs=VMEM,
-            scratch_shapes=[
-                pltpu.VMEM((1, width), jnp.float32),
-                pltpu.VMEM((width, rays + LANES), jnp.float32),
-            ],
-            compiler_params=ALONE if turn is None else LIMIT,
+            scratch_shapes=[pltpu.VMEM((1, width), jnp.float32)],
+            compiler_params=LIMIT,
             name="pack",
         )(*given)
         return lax.all_to_all(
@@ -363,7 +378,7 @@
                 pltpu.VMEM((2 * tiles, 8, rays + LANES), jnp.float32),
                 pltpu.SMEM((4 * (2 * tiles * ROOM + 1),), jnp.int32),
                 pltpu.VMEM((2, 2 * BATCH, rays), jnp.float32),
-                pltpu.VMEM((2, 2 * BATCH, LANES), jnp.float32),
+                pltpu.VMEM((2 * BATCH, LANES), jnp.float32),
                 pltpu.VMEM((8, 2 * BATCH, rays), jnp.float32),
             ],
             compiler_params=LIMIT,

time: 27.8 us -> 28 us (level); the launches traced: 27.7 us -> 28.4 us
  local copies, waits for them, and re-layouts: 0.01 us -> 1.46 us
  Pallas kernels: 8.64 us -> 8.14 us
    pallas_call x1, Pallas kernels: 2.23 us -> 0.7 us  [exchange(): pl.pallas_call(kernel, out_shape=jax.ShapeDtypeStruct((8 * tiles, rays +...]
    unnamed x6 -> x8, local copies, waits for them, and re-layouts: 0.01 us -> 1.46 us
    pallas_call x1, Pallas kernels: 6.41 us -> 7.12 us  [deposit(): pl.pallas_call(kernel, out_shape=(jax.ShapeDtypeStruct((TILE, TILE), jnp....]
    pallas_call x0 -> x1, Pallas kernels: none -> 0.32 us  [exchange(): pl.pallas_call(lay_kernel, out_shape=(jax.ShapeDtypeStruct((3, width, ray...]
where the time goes in v1:
time: 28 us; the launch traced here: 28.4 us
  blocking collectives  16.6 us (59%)
  Pallas kernels  8.14 us (29%)
  local copies, waits for them, and re-layouts  1.46 us (5%)
  starting transfers between devices  0.82 us (3%)
  between operations  0.72 us (3%)
  other arithmetic  0.69 us (2%)
    all_to_all x1, blocking collectives, exchange(): lax.all_to_all(outgoing.reshape(tiles, 8, rays + LANES), ('row', 'col'),...  16.6 us
    pallas_call x1, Pallas kernels, deposit(): pl.pallas_call(kernel, out_shape=(jax.ShapeDtypeStruct((TILE, TILE), jnp....  7.12 us
    unnamed x8, local copies, waits for them, and re-layouts  1.46 us
    ppermute x1, starting transfers between devices, deposit(): other = lax.ppermute(mine, 'row', [(i, i ^ 1) for i in range(row_count)])  0.82 us
    pallas_call x1, Pallas kernels, exchange(): pl.pallas_call(kernel, out_shape=jax.ShapeDtypeStruct((8 * tiles, rays +...  0.7 us
    reduce_max x1, other arithmetic, shards(): turns = jnp.max(mine[:, 7, 2 * LANES + COUNT]).astype(jnp.int32)  0.69 us
  transfers between devices with their start and end apart: 1, of which 0 were waited for; matrix products, arithmetic and copies ran while one was open for 2% of the time, Pallas kernels for 0%

profile of v1, /device:TPU:1, one launch (start us, length us, event | category | flops | bytes accessed | tf_op | source)
XLA Modules:
  0.0 28.4 jit_solution(17762159094503498354)
XLA Ops:
  0.0 0.0 copy-start
  0.0 0.8 %copy-done = f32[16,2,384]{2,1,0:T(2,128)S(1)} copy-done((f32[16,2,384]{2,1,0:T(2,128)S(1)}, f32[16,2,384]{2,1,0:T(2,128)}, u32[]{:S(2)}) %copy-start) | copy-done | bytes 49176
  0.8 0.3 %lay.2 = (bf16[3,128,512]{2,1,0:T(8,128)(2,1)S(1)}, f32[4,128]{1,0:T(4,128)S(1)}) custom-call(f32[16,2,384]{2,1,0:T(2,128)S(1)} %copy-done), custom_call_target="tpu_custom_call" | custom-call | tf_op jit(solution)/shard_map/lay/pallas_call | solution.py:330
  1.1 0.0 copy-start.2
  1.1 0.6 %copy-done.2 = s32[16,1]{0,1:T(1,128)S(1)} copy-done((s32[16,1]{0,1:T(1,128)S(1)}, s32[16,1]{0,1:T(1,128)}, u32[]{:S(2)}) %copy-start.2) | copy-done | bytes 88
  1.8 0.7 %pack.2 = f32[128,512]{1,0:T(8,128)S(1)} custom-call(s32[1,16]{1,0:T(1,128)S(1)} %bitcast.10, bf16[3,128,512]{2,1,0:T(8,128)(2,1)S(1)} %get-tuple-element.54.parts_ref, f32[4,128]{1,0:T(4,128)S(1)} %get-tuple-element.55.bounds_ref), custom_call_target="tpu_custom_call" | custom-call | tf_op jit(solution)/shard_map/pack/pallas_call | solution.py:344
  2.5 0.0 copy-start.1
  2.5 0.0 copy-start.3
  2.5 16.6 %all_to_all.11.refs_0_ = f32[16,8,512]{2,1,0:T(8,128)S(1)} all-to-all(f32[16,8,512]{2,1,0:T(8,128)S(1)} %bitcast.9), channel_id=1, replica_groups=mesh['maps'=2,'row'=4,'col'=4] {'row','col'}, dimensions={0} | all-to-all | bytes 524288 | tf_op jit(solution)/shard_map/all_to_all | solution.py:353
  19.1 0.8 %collective-permute-start.1 = (f32[16,8,512]{2,1,0:T(8,128)S(1)}, f32[16,8,512]{2,1,0:T(8,128)S(1)}, u32[]{:S(2)}, u32[]{:S(2)}) collective-permute-start(f32[16,8,512]{2,1,0:T(8,128)S(1)} %all_to_all.11.refs_0_), channel_id=1, source_target_pairs={{0,4},{4,0},{8,12},{12,8},{1,5},{5,1},{9,13},{13,9},{2,6},{6,2},{1... | collective-permute-start | bytes 786440 | tf_op jit(solution)/shard_map/ppermute | solution.py:358
  19.9 0.7 %slice_reduce_fusion = f32[]{:T(128)} fusion(f32[16,8,512]{2,1,0:T(8,128)S(1)} %all_to_all.11.refs_0_), kind=kLoop, calls=%fused_computation | loop fusion | flops 15 | bytes 68 | tf_op jit(solution)/shard_map/reduce_max | solution.py:389
  21.3 0.0 collective-permute-done.1.refs_1_
  21.3 0.0 copy-done.1
  21.3 0.0 copy-done.3
  21.3 7.1 %spread.2 = (f32[128,128]{1,0:T(8,128)}, f32[192,192]{1,0:T(8,128)S(1)}, s32[1,16]{1,0:T(1,128)S(1)}, f32[16,2,384]{2,1,0:T(2,128)S(1)}) custom-call(f32[16,8,512]{2,1,0:T(8,128)S(1)} %all_to_all.11.refs_0_, f32[16,8,512]{2,1,0:T(8,128)S(1)} %collective-permute-done.1.refs_1_, f32[65,65]{1,0:T(8,128)S(1)} %copy-done.3, s32[1,16]{1,0:T(1,128)S(1)} %bitcast.11, ...), custom_call_target="tpu_custom_call" | custom-call | tf_op jit(solution)/shard_map/spread/pallas_call | solution.py:364
  (1 shorter events, 0.0 us)
Async XLA Ops:
  0.0 0.8 %copy-start = (f32[16,2,384]{2,1,0:T(2,128)S(1)}, f32[16,2,384]{2,1,0:T(2,128)}, u32[]{:S(2)}) copy-start(f32[16,2,384]{2,1,0:T(2,128)} %refs_4_.1) | copy-start | bytes 147460
  1.1 0.7 %copy-start.2 = (s32[16,1]{0,1:T(1,128)S(1)}, s32[16,1]{0,1:T(1,128)}, u32[]{:S(2)}) copy-start(s32[16,1]{0,1:T(1,128)} %param.6) | copy-start | bytes 196
  2.5 18.8 %copy-start.1 = (f32[16,2,384]{2,1,0:T(2,128)S(1)}, f32[16,2,384]{2,1,0:T(2,128)}, u32[]{:S(2)}) copy-start(f32[16,2,384]{2,1,0:T(2,128)} %refs_4_.1) | copy-start | bytes 147460
  2.5 18.8 %copy-start.3 = (f32[65,65]{1,0:T(8,128)S(1)}, f32[65,65]{1,0:T(8,128)}, u32[]{:S(2)}) copy-start(f32[65,65]{1,0:T(8,128)} %refs_2_.1) | copy-start | bytes 50704
  19.1 2.2 %collective-permute-start.1 = (f32[16,8,512]{2,1,0:T(8,128)S(1)}, f32[16,8,512]{2,1,0:T(8,128)S(1)}, u32[]{:S(2)}, u32[]{:S(2)}) collective-permute-start(f32[16,8,512]{2,1,0:T(8,128)S(1)} %all_to_all.11.refs_0_), channel_id=1, source_target_pairs={{0,4},{4,0},{8,12},{12,8},{1,5},{5,1},{9,13},{13,9},{2,6},{6,2},{1... | collective-permute-start | bytes 786440 | tf_op jit(solution)/shard_map/ppermute | solution.py:358
